TPU v7x, 32 devices: a whole 2x2x4 slice. The times are simulated.
32 devices in a mesh: gx: 4 (over z), gy: 2 (over y), gz: 4 (over x, core).
Axes of the slice: x: 2, y: 2, z: 4, core: 2. Of those that a mesh axis runs over, the one named last changes fastest.
Arguments:
- residual: float32 [64, 32, 512], P('gx', 'gy', 'gz'), may hold values from -6 to 6
- solution: float32 [64, 32, 512], P('gx', 'gy', 'gz'), may hold values from -6 to 6
- direction: float32 [64, 32, 512], P('gx', 'gy', 'gz'), may hold values from -6 to 6
- conductance: float32 [3, 64, 32, 512], P(None, 'gx', 'gy', 'gz'), may hold values from 0.3 to 3
- mass_term: float32 [64, 32, 512], P('gx', 'gy', 'gz'), may hold values from 0.2 to 1
- eigen_basis: float32 [10, 10], replicated, may hold values from -2 to 2
- inverse_eigen_sums: float32 [80, 40, 640], P('gx', 'gy', 'gz'), may hold values from 0.1 to 1
- element_coarse_index: int32 [8, 4, 64], P('gx', 'gy', 'gz'), may hold values from 0 to 63
- xxt_values: float32 [256, 64, 128], P(('gx', 'gy', 'gz')), may hold values from -0.0625 to 0.0625
- xxt_blocks: int32 [256], P(('gx', 'gy', 'gz')), may hold values from 0 to 15
- prior_inner: float32 [1], replicated, may hold values from 409600 to 1638400
Outputs:
- new_solution: float32 [64, 32, 512], P('gx', 'gy', 'gz')
- new_residual: float32 [64, 32, 512], P('gx', 'gy', 'gz')
- new_direction: float32 [64, 32, 512], P('gx', 'gy', 'gz')
Inputs may be any that keep to these rules, and one draw needn't show every extreme that they name: `element_coarse_index`: an element's coarse unknown is one of the 64 of the device that holds the element. `xxt_blocks`: block numbers of the coarse vector, repeats allowed.
All inputs are finite; a program needn't handle non-finite values.
Results may differ from a plain program's by a relative error of at most 0.00011.
Values sent between devices are 32-bit elements; how exact they have to be, the bound alone decides.
A program may use at most 64 MiB of HBM per device.

v0:
```python
import jax
import jax.numpy as jnp
import numpy as np
from jax import lax
from jax.sharding import PartitionSpec as P

HIGH = lax.Precision.HIGHEST


def padded_2(block, sides, width):
    for axis, dim in sides:
        count = lax.axis_size(axis)
        forward = [(i, i + 1) for i in range(count - 1)]
        backward = [(target, source) for source, target in forward]
        low = lax.ppermute(
            lax.slice_in_dim(block, block.shape[dim] - width, None, axis=dim), axis, forward
        )
        high = lax.ppermute(lax.slice_in_dim(block, 0, width, axis=dim), axis, backward)
        block = jnp.concatenate([low, block, high], axis=dim)
    return block


def cheb_matrix():
    count = 8
    points = np.cos(np.pi * np.arange(count) / (count - 1))
    signs = np.array([2.0, 1, 1, 1, 1, 1, 1, 2.0]) * (-1.0) ** np.arange(count)
    differ = points[:, None] - points[None, :] + np.eye(count)
    matrix = np.outer(signs, 1.0 / signs) / differ
    matrix = matrix - np.eye(count) * np.sum(matrix, axis=1)[:, None]
    return (0.25 * matrix).astype(np.float32)


def extended_index(count):
    parts = [
        np.array(
            [8 * element] + list(range(8 * element + 2, 8 * element + 10)) + [8 * element + 11]
        )
        for element in range(count)
    ]
    return np.concatenate(parts).astype(np.int32)


def inside_index(count):
    parts = [np.arange(10 * element + 1, 10 * element + 9) for element in range(count)]
    return np.concatenate(parts).astype(np.int32)


def assemble_padded(padded):
    result = padded
    for which_axis in range(3):
        length = result.shape[which_axis] - 2
        position = np.arange(length) % 8
        shape_list = [1, 1, 1]
        shape_list[which_axis] = length
        upper = jnp.asarray((position == 7).astype(np.float32).reshape(shape_list))
        lower = jnp.asarray((position == 0).astype(np.float32).reshape(shape_list))
        centre = lax.slice_in_dim(result, 1, length + 1, axis=which_axis)
        above = lax.slice_in_dim(result, 2, length + 2, axis=which_axis)
        below = lax.slice_in_dim(result, 0, length, axis=which_axis)
        result = centre + upper * above + lower * below
    return result


def apply_big(matrix, values, which_axis):
    if which_axis == 0:
        return jnp.einsum("ij,jyz->iyz", matrix, values, precision=HIGH)
    if which_axis == 1:
        return jnp.einsum("ij,xjz->xiz", matrix, values, precision=HIGH)
    return jnp.einsum("ij,xyj->xyi", matrix, values, precision=HIGH)


def local_operator(values, conductance, mass_term, tables):
    total = mass_term * values
    for which_axis in range(3):
        grad = apply_big(tables[which_axis], values, which_axis)
        total = total + apply_big(tables[which_axis].T, conductance[which_axis] * grad, which_axis)
    return total


def aggregate_table(count):
    return jnp.asarray(
        (np.arange(8 * count)[:, None] // 8 == np.arange(count)[None, :]).astype(np.float32)
    )


def body(
    residual,
    solution,
    direction,
    conductance,
    mass_term,
    eigen_basis,
    inverse_eigen_sums,
    element_coarse_index,
    xxt_values,
    xxt_blocks,
    prior_inner,
):
    elems_x = residual.shape[0] // 8
    elems_y = residual.shape[1] // 8
    elems_z = residual.shape[2] // 8
    counts = (elems_x, elems_y, elems_z)
    base = cheb_matrix()
    tables = tuple(
        (jnp.asarray(np.kron(np.eye(count_one, dtype=np.float32), base)) for count_one in counts)
    )
    device_count = lax.axis_size("gx") * lax.axis_size("gy") * lax.axis_size("gz")
    padded = padded_2(residual, (("gx", 0), ("gy", 1), ("gz", 2)), 2)
    extended_element = jnp.take(padded, jnp.asarray(extended_index(elems_x)), axis=0)
    extended_element = jnp.take(extended_element, jnp.asarray(extended_index(elems_y)), axis=1)
    extended_element = jnp.take(extended_element, jnp.asarray(extended_index(elems_z)), axis=2)
    bases = tuple(
        (jnp.kron(jnp.eye(count_one, dtype=jnp.float32), eigen_basis) for count_one in counts)
    )
    spectral = extended_element
    for which_axis in range(3):
        spectral = apply_big(bases[which_axis].T, spectral, which_axis)
    spectral = inverse_eigen_sums * spectral
    for which_axis in range(3):
        spectral = apply_big(bases[which_axis], spectral, which_axis)
    device_portion = jnp.take(spectral, jnp.asarray(inside_index(elems_x)), axis=0)
    device_portion = jnp.take(device_portion, jnp.asarray(inside_index(elems_y)), axis=1)
    device_portion = jnp.take(device_portion, jnp.asarray(inside_index(elems_z)), axis=2)
    inner_local = jnp.sum(extended_element * spectral)
    agg_x = aggregate_table(elems_x)
    agg_y = aggregate_table(elems_y)
    agg_z = aggregate_table(elems_z)
    summed = jnp.einsum("xyz,zc->xyc", residual, agg_z, precision=HIGH)
    summed = jnp.einsum("xyc,yb->xbc", summed, agg_y, precision=HIGH)
    element_sum = jnp.einsum("xbc,xa->abc", summed, agg_x, precision=HIGH)
    coarse_count = xxt_values.shape[1]
    block_size = xxt_values.shape[2]
    onehot_ids = (
        element_coarse_index[..., None] == jnp.arange(coarse_count, dtype=jnp.int32)
    ).astype(jnp.float32)
    coarse_residual = jnp.einsum("abcn,abc->n", onehot_ids, element_sum, precision=HIGH)
    contrib = jnp.einsum("knb,n->kb", xxt_values, coarse_residual, precision=HIGH)
    block_count = coarse_count * device_count // block_size
    partial_inner = jnp.zeros((block_count, block_size), jnp.float32).at[xxt_blocks].add(contrib)
    coarse_inner, inner_sum = lax.psum((partial_inner, inner_local), ("gx", "gy", "gz"))
    coarse_solution = jnp.einsum("knb,kb->n", xxt_values, coarse_inner[xxt_blocks], precision=HIGH)
    element_coarse = jnp.einsum("abcn,n->abc", onehot_ids, coarse_solution, precision=HIGH)
    spread_values = jnp.einsum("abc,xa->xbc", element_coarse, agg_x, precision=HIGH)
    spread_values = jnp.einsum("xbc,yb->xyc", spread_values, agg_y, precision=HIGH)
    spread_values = jnp.einsum("xyc,zc->xyz", spread_values, agg_z, precision=HIGH)
    preconditioned = device_portion + spread_values
    inner = inner_sum + jnp.sum(coarse_inner * coarse_inner)
    ratio = inner / prior_inner[0]
    new_direction = preconditioned + ratio * direction
    image = local_operator(new_direction, conductance, mass_term, tables)
    curvature = lax.psum(jnp.sum(new_direction * image), ("gx", "gy", "gz"))
    alpha = inner / curvature
    new_solution = solution + alpha * new_direction
    image_padded = padded_2(image, (("gx", 0), ("gy", 1), ("gz", 2)), 1)
    new_residual = residual - alpha * assemble_padded(image_padded)
    return (new_solution, new_residual, new_direction)


def solution(mesh):
    in_specs = (
        P("gx", "gy", "gz"),
        P("gx", "gy", "gz"),
        P("gx", "gy", "gz"),
        P(None, "gx", "gy", "gz"),
        P("gx", "gy", "gz"),
        P(),
        P("gx", "gy", "gz"),
        P("gx", "gy", "gz"),
        P(("gx", "gy", "gz"), None, None),
        P(("gx", "gy", "gz")),
        P(),
    )
    out_specs = (P("gx", "gy", "gz"), P("gx", "gy", "gz"), P("gx", "gy", "gz"))
    return jax.shard_map(body, mesh=mesh, in_specs=in_specs, out_specs=out_specs, check_vma=False)
```

profile of v0, /device:TPU:6, one launch (start us, length us, event | category | flops | bytes accessed | tf_op | source)
XLA Modules:
  0.0 164.0 jit_solution(628046587861280396)
XLA Ops:
  0.7 0.8 fusion.36
  1.6 3.5 %collective-permute-start = (f32[2,16,128]{2,1,0:T(8,128)S(1)}, f32[2,16,128]{2,1,0:T(8,128)S(1)}, u32[]{:S(2)}, u32[]{:S(2)}) collective-permute-start(f32[2,16,128]{2,1,0:T(8,128)S(1)} %get-tuple-element.16), channel_id=1, source_target_pairs={{0,8},{8,16},{16,24},{1,9},{9,17},{17,25},{2,10},{10,18},{18,26},{... | collective-permute-start | bytes 49160 | tf_op jit(solution)/shard_map/ppermute | solution.py:15
  5.0 1.3 collective-permute-start.1
  7.0 1.9 %convolution_bitcast_fusion.4 = f32[16,16,16]{1,2,0:T(8,128)S(1)} fusion(f32[128,16,1]{0,1,2:T(8,128)} %constant.176, f32[16,16,128]{2,1,0:T(8,128)} %param.29), kind=kOutput, calls=%fused_computation.19 | convolution fusion | flops 6291456 | bytes 155648 | tf_op jit(solution)/shard_map/xyz,zc->xyc/dot_general | solution.py:128
  9.0 1.7 %convolution_bitcast_fusion.6 = f32[16,2,16]{2,1,0:T(2,128)S(1)} fusion(f32[16,16,16]{1,2,0:T(8,128)S(1)} %convolution_bitcast_fusion.4, f32[16,2,1]{0,1,2:T(2,128)} %constant.175), kind=kOutput, calls=%fused_computation.22 | convolution fusion | flops 98304 | bytes 18560 | tf_op jit(solution)/shard_map/xyc,yb->xbc/dot_general | solution.py:129
  10.7 0.8 convolution_bitcast_fusion.7
  12.3 0.8 broadcast_multiply_fusion
  13.7 2.4 %collective-permute-start.3 = (f32[20,2,128]{2,1,0:T(2,128)S(1)}, f32[20,2,128]{2,1,0:T(2,128)S(1)}, u32[]{:S(2)}, u32[]{:S(2)}) collective-permute-start(f32[20,2,128]{2,1,0:T(2,128)S(1)} %get-tuple-element.10), channel_id=1, source_target_pairs={{4,0},{5,1},{6,2},{7,3},{12,8},{13,9},{14,10},{15,11},{20,16},{21,... | collective-permute-start | bytes 61448 | tf_op jit(solution)/shard_map/ppermute | solution.py:18
  16.2 1.3 collective-permute-start.2
  17.6 4.2 %collective-permute-done.2 = f32[20,2,128]{2,1,0:T(2,128)S(1)} collective-permute-done((f32[20,2,128]{2,1,0:T(2,128)S(1)}, f32[20,2,128]{2,1,0:T(2,128)S(1)}, u32[]{:S(2)}, u32[]{:S(2)}) %collective-permute-start.2) | collective-permute-done | bytes 20512 | tf_op jit(solution)/shard_map/ppermute | solution.py:15
  22.0 1.9 %collective-permute-start.5 = (f32[20,20,2]{2,1,0:T(8,128)S(1)}, f32[20,20,2]{2,1,0:T(8,128)S(1)}, u32[]{:S(2)}, u32[]{:S(2)}) collective-permute-start(f32[20,20,2]{2,1,0:T(8,128)S(1)} %get-tuple-element.6), channel_id=1, source_target_pairs={{1,0},{2,1},{3,2},{5,4},{6,5},{7,6},{9,8},{10,9},{11,10},{13,12},{... | collective-permute-start | bytes 9608 | tf_op jit(solution)/shard_map/ppermute | solution.py:18
  23.9 2.4 %collective-permute-start.4 = (f32[20,20,2]{2,1,0:T(8,128)S(1)}, f32[20,20,2]{2,1,0:T(8,128)S(1)}, u32[]{:S(2)}, u32[]{:S(2)}) collective-permute-start(f32[20,20,2]{2,1,0:T(8,128)S(1)} %get-tuple-element.5), channel_id=1, source_target_pairs={{0,1},{1,2},{2,3},{4,5},{5,6},{6,7},{8,9},{9,10},{10,11},{12,13},{... | collective-permute-start | bytes 9608 | tf_op jit(solution)/shard_map/ppermute | solution.py:15
  28.5 3.0 %collective-permute-done.4 = f32[20,20,2]{2,1,0:T(8,128)S(1)} collective-permute-done((f32[20,20,2]{2,1,0:T(8,128)S(1)}, f32[20,20,2]{2,1,0:T(8,128)S(1)}, u32[]{:S(2)}, u32[]{:S(2)}) %collective-permute-start.4) | collective-permute-done | bytes 3232 | tf_op jit(solution)/shard_map/ppermute | solution.py:15
  33.1 2.2 %copy.42 = f32[20,20,132]{1,0,2:T(8,128)} copy(f32[20,20,132]{2,0,1:T(8,128)S(1)} %bitcast.107) | data formatting | bytes 422400 | tf_op jit(solution)/shard_map/jit(_take)/gather | solution.py:110
  35.3 2.1 %gather_fusion.2 = f32[160,20,20]{2,1,0:T(8,128)S(1)} fusion(f32[20,20,132]{1,0,2:T(8,128)} %copy.42, s32[1024]{0:T(1024)S(1)} %pad_clamp_fusion.3), kind=kCustom, calls=%fused_computation.2 | custom fusion | bytes 512640 | tf_op jit(solution)/shard_map/jit(_take)/gather | solution.py:111
  37.4 0.8 copy.43
  38.2 1.0 copy.45
  42.4 1.2 fusion.3
  43.5 41.6 %all-reduce = (f32[16,128]{1,0:T(8,128)S(1)}, f32[]{:T(128)}) all-reduce(f32[16,128]{1,0:T(8,128)S(1)} %scatter_custom_fusion, f32[]{:T(128)} %get-tuple-element.17), channel_id=1, replica_groups=mesh['gx'=4,'gy'=2,'gz'=4] {'gx','gy','gz'}, use_global_device_ids=true, to_apply=%region_3.4 | all-reduce | flops 2049 | bytes 16392 | tf_op jit(solution)/shard_map/psum | solution.py:140
  87.1 1.1 convolution_bitcast_fusion.5
  92.8 1.4 fusion.2
  95.7 0.9 multiply_reduce_fusion
  96.6 1.3 collective-permute-start.7
  97.9 4.5 %collective-permute-start.6 = (f32[1,16,128]{2,1,0:T(8,128)S(1)}, f32[1,16,128]{2,1,0:T(8,128)S(1)}, u32[]{:S(2)}, u32[]{:S(2)}) collective-permute-start(f32[1,16,128]{2,1,0:T(8,128)S(1)} %get-tuple-element.13), channel_id=1, source_target_pairs={{0,8},{8,16},{16,24},{1,9},{9,17},{17,25},{2,10},{10,18},{18,26},{... | collective-permute-start | bytes 24584 | tf_op jit(solution)/shard_map/ppermute | solution.py:15
  102.4 1.3 collective-permute-done.6
  103.8 3.6 %collective-permute-start.9 = (f32[18,1,128]{2,1,0:T(1,128)S(1)}, f32[18,1,128]{2,1,0:T(1,128)S(1)}, u32[]{:S(2)}, u32[]{:S(2)}) collective-permute-start(f32[18,1,128]{2,1,0:T(1,128)S(1)} %get-tuple-element.12), channel_id=1, source_target_pairs={{4,0},{5,1},{6,2},{7,3},{12,8},{13,9},{14,10},{15,11},{20,16},{21,... | collective-permute-start | bytes 27656 | tf_op jit(solution)/shard_map/ppermute | solution.py:18
  107.4 1.3 collective-permute-start.8
  108.7 43.5 %psum.23 = f32[]{:T(128)} all-reduce(f32[]{:T(128)} %get-tuple-element.19), channel_id=1, replica_groups=mesh['gx'=4,'gy'=2,'gz'=4] {'gx','gy','gz'}, use_global_device_ids=true, to_apply=%region_6.7 | all-reduce | flops 1 | bytes 8 | tf_op jit(solution)/shard_map/psum | solution.py:151
  153.0 1.9 %collective-permute-start.11 = (f32[18,18,1]{2,1,0:T(8,128)S(1)}, f32[18,18,1]{2,1,0:T(8,128)S(1)}, u32[]{:S(2)}, u32[]{:S(2)}) collective-permute-start(f32[18,18,1]{2,1,0:T(8,128)S(1)} %get-tuple-element.8), channel_id=1, source_target_pairs={{1,0},{2,1},{3,2},{5,4},{6,5},{7,6},{9,8},{10,9},{11,10},{13,12},{... | collective-permute-start | bytes 3896 | tf_op jit(solution)/shard_map/ppermute | solution.py:18
  155.0 2.4 %collective-permute-start.10 = (f32[18,18,1]{2,1,0:T(8,128)S(1)}, f32[18,18,1]{2,1,0:T(8,128)S(1)}, u32[]{:S(2)}, u32[]{:S(2)}) collective-permute-start(f32[18,18,1]{2,1,0:T(8,128)S(1)} %get-tuple-element.7), channel_id=1, source_target_pairs={{0,1},{1,2},{2,3},{4,5},{5,6},{6,7},{8,9},{9,10},{10,11},{12,13},{... | collective-permute-start | bytes 3896 | tf_op jit(solution)/shard_map/ppermute | solution.py:15
  158.4 3.8 %collective-permute-done.10 = f32[18,18,1]{2,1,0:T(8,128)S(1)} collective-permute-done((f32[18,18,1]{2,1,0:T(8,128)S(1)}, f32[18,18,1]{2,1,0:T(8,128)S(1)}, u32[]{:S(2)}, u32[]{:S(2)}) %collective-permute-start.10) | collective-permute-done | bytes 1328 | tf_op jit(solution)/shard_map/ppermute | solution.py:15
  163.2 0.8 fusion.14
  (103 shorter events, 17.2 us)
Async XLA Ops:
  0.6 12.7 %copy-start = (f32[8,64,128]{2,1,0:T(8,128)S(1)}, f32[8,64,128]{2,1,0:T(8,128)}, u32[]{:S(2)}) copy-start(f32[8,64,128]{2,1,0:T(8,128)} %param.37) | copy-start | bytes 786436
  0.6 12.9 %copy-start.15 = (s32[128]{0:T(128)S(1)}, s32[128]{0:T(128)}, u32[]{:S(2)}) copy-start(s32[128]{0:T(128)} %constant.174) | copy-start | bytes 1540
  0.7 12.9 %copy-start.16 = (s32[16]{0:T(128)S(1)}, s32[16]{0:T(128)}, u32[]{:S(2)}) copy-start(s32[16]{0:T(128)} %constant.172) | copy-start | bytes 196
  0.7 13.0 %copy-start.14 = (s32[20]{0:T(128)S(1)}, s32[20]{0:T(128)}, u32[]{:S(2)}) copy-start(s32[20]{0:T(128)} %constant.169) | copy-start | bytes 244
  0.7 13.0 %copy-start.2 = (f32[16,16,128]{2,1,0:T(8,128)S(1)}, f32[16,16,128]{2,1,0:T(8,128)}, u32[]{:S(2)}) copy-start(f32[16,16,128]{2,1,0:T(8,128)} %param.29) | copy-start | bytes 393220
  0.7 12.4 %copy-start.19 = (s32[2,2,16]{2,1,0:T(2,128)S(1)}, s32[2,2,16]{2,1,0:T(2,128)}, u32[]{:S(2)}) copy-start(s32[2,2,16]{2,1,0:T(2,128)} %param.36) | copy-start | bytes 772
  1.6 12.1 %collective-permute-start = (f32[2,16,128]{2,1,0:T(8,128)S(1)}, f32[2,16,128]{2,1,0:T(8,128)S(1)}, u32[]{:S(2)}, u32[]{:S(2)}) collective-permute-start(f32[2,16,128]{2,1,0:T(8,128)S(1)} %get-tuple-element.16), channel_id=1, source_target_pairs={{0,8},{8,16},{16,24},{1,9},{9,17},{17,25},{2,10},{10,18},{18,26},{... | collective-permute-start | bytes 49160 | tf_op jit(solution)/shard_map/ppermute | solution.py:15
  5.0 8.7 %collective-permute-start.1 = (f32[2,16,128]{2,1,0:T(8,128)S(1)}, f32[2,16,128]{2,1,0:T(8,128)S(1)}, u32[]{:S(2)}, u32[]{:S(2)}) collective-permute-start(f32[2,16,128]{2,1,0:T(8,128)S(1)} %get-tuple-element.15), channel_id=1, source_target_pairs={{8,0},{16,8},{24,16},{9,1},{17,9},{25,17},{10,2},{18,10},{26,18},{... | collective-permute-start | bytes 49160 | tf_op jit(solution)/shard_map/ppermute | solution.py:18
  6.3 11.1 %copy-start.13 = (s32[160]{0:T(256)S(1)}, s32[160]{0:T(256)}, u32[]{:S(2)}) copy-start(s32[160]{0:T(256)} %constant.171) | copy-start | bytes 1924
  13.7 3.9 %collective-permute-start.3 = (f32[20,2,128]{2,1,0:T(2,128)S(1)}, f32[20,2,128]{2,1,0:T(2,128)S(1)}, u32[]{:S(2)}, u32[]{:S(2)}) collective-permute-start(f32[20,2,128]{2,1,0:T(2,128)S(1)} %get-tuple-element.10), channel_id=1, source_target_pairs={{4,0},{5,1},{6,2},{7,3},{12,8},{13,9},{14,10},{15,11},{20,16},{21,... | collective-permute-start | bytes 61448 | tf_op jit(solution)/shard_map/ppermute | solution.py:18
  16.2 5.7 %collective-permute-start.2 = (f32[20,2,128]{2,1,0:T(2,128)S(1)}, f32[20,2,128]{2,1,0:T(2,128)S(1)}, u32[]{:S(2)}, u32[]{:S(2)}) collective-permute-start(f32[20,2,128]{2,1,0:T(2,128)S(1)} %get-tuple-element.9), channel_id=1, source_target_pairs={{0,4},{1,5},{2,6},{3,7},{8,12},{9,13},{10,14},{11,15},{16,20},{17,... | collective-permute-start | bytes 61448 | tf_op jit(solution)/shard_map/ppermute | solution.py:15
  22.0 6.4 %collective-permute-start.5 = (f32[20,20,2]{2,1,0:T(8,128)S(1)}, f32[20,20,2]{2,1,0:T(8,128)S(1)}, u32[]{:S(2)}, u32[]{:S(2)}) collective-permute-start(f32[20,20,2]{2,1,0:T(8,128)S(1)} %get-tuple-element.6), channel_id=1, source_target_pairs={{1,0},{2,1},{3,2},{5,4},{6,5},{7,6},{9,8},{10,9},{11,10},{13,12},{... | collective-permute-start | bytes 9608 | tf_op jit(solution)/shard_map/ppermute | solution.py:18
  23.9 7.5 %collective-permute-start.4 = (f32[20,20,2]{2,1,0:T(8,128)S(1)}, f32[20,20,2]{2,1,0:T(8,128)S(1)}, u32[]{:S(2)}, u32[]{:S(2)}) collective-permute-start(f32[20,20,2]{2,1,0:T(8,128)S(1)} %get-tuple-element.5), channel_id=1, source_target_pairs={{0,1},{1,2},{2,3},{4,5},{5,6},{6,7},{8,9},{9,10},{10,11},{12,13},{... | collective-permute-start | bytes 9608 | tf_op jit(solution)/shard_map/ppermute | solution.py:15
  39.2 1.3 copy-start.4
  41.7 45.2 %copy-start.10 = (f32[16,2,1]{0,1,2:T(2,128)S(1)}, f32[16,2,1]{0,1,2:T(2,128)}, u32[]{:S(2)}) copy-start(f32[16,2,1]{0,1,2:T(2,128)} %constant.175) | copy-start | bytes 388
  89.5 3.3 %copy-start.9 = (f32[128,16,1]{0,1,2:T(8,128)S(1)}, f32[128,16,1]{0,1,2:T(8,128)}, u32[]{:S(2)}) copy-start(f32[128,16,1]{0,1,2:T(8,128)} %constant.176) | copy-start | bytes 24580
  90.2 4.0 %copy-start.3 = (f32[3,16,16,128]{3,2,1,0:T(8,128)S(1)}, f32[3,16,16,128]{3,2,1,0:T(8,128)}, u32[]{:S(2)}) copy-start(f32[3,16,16,128]{3,2,1,0:T(8,128)} %param.32) | copy-start | bytes 1179652
  90.2 4.0 %copy-start.8 = (f32[16,16,1]{1,0,2:T(8,128)S(1)}, f32[16,16,1]{1,0,2:T(8,128)}, u32[]{:S(2)}) copy-start(f32[16,16,1]{1,0,2:T(8,128)} %constant.177) | copy-start | bytes 3076
  90.2 4.2 %slice-start = ((f32[3,16,16,128]{3,2,1,0:T(8,128)}), f32[1,16,16,128]{3,2,1,0:T(8,128)S(1)}, s32[]{:S(2)}) async-start(f32[3,16,16,128]{3,2,1,0:T(8,128)} %param.32), calls=%async_computation | async-start | bytes 262144 | tf_op jit(solution)/shard_map/slice | solution.py:76
  91.0 4.1 %copy-start.5 = (f32[128,128,1]{1,0,2:T(8,128)S(1)}, f32[128,128,1]{1,0,2:T(8,128)}, u32[]{:S(2)}) copy-start(f32[128,128,1]{1,0,2:T(8,128)} %constant.178) | copy-start | bytes 196612
  91.4 4.0 %copy-start.7 = (f32[16,16,128]{2,1,0:T(8,128)S(1)}, f32[16,16,128]{2,1,0:T(8,128)}, u32[]{:S(2)}) copy-start(f32[16,16,128]{2,1,0:T(8,128)} %param.33) | copy-start | bytes 393220
  94.2 63.2 %copy-start.1 = (f32[16,16,128]{2,1,0:T(8,128)}, f32[16,16,128]{2,1,0:T(8,128)S(1)}, u32[]{:S(2)}) copy-start(f32[16,16,128]{2,1,0:T(8,128)S(1)} %fusion.2) | copy-start | bytes 393220
  95.4 62.0 %copy-start.6 = (f32[16,16,128]{2,1,0:T(8,128)S(1)}, f32[16,16,128]{2,1,0:T(8,128)}, u32[]{:S(2)}) copy-start(f32[16,16,128]{2,1,0:T(8,128)} %param.30) | copy-start | bytes 393220
  96.6 5.8 %collective-permute-start.7 = (f32[1,16,128]{2,1,0:T(8,128)S(1)}, f32[1,16,128]{2,1,0:T(8,128)S(1)}, u32[]{:S(2)}, u32[]{:S(2)}) collective-permute-start(f32[1,16,128]{2,1,0:T(8,128)S(1)} %get-tuple-element.14), channel_id=1, source_target_pairs={{8,0},{16,8},{24,16},{9,1},{17,9},{25,17},{10,2},{18,10},{26,18},{... | collective-permute-start | bytes 24584 | tf_op jit(solution)/shard_map/ppermute | solution.py:18
  97.9 5.9 %collective-permute-start.6 = (f32[1,16,128]{2,1,0:T(8,128)S(1)}, f32[1,16,128]{2,1,0:T(8,128)S(1)}, u32[]{:S(2)}, u32[]{:S(2)}) collective-permute-start(f32[1,16,128]{2,1,0:T(8,128)S(1)} %get-tuple-element.13), channel_id=1, source_target_pairs={{0,8},{8,16},{16,24},{1,9},{9,17},{17,25},{2,10},{10,18},{18,26},{... | collective-permute-start | bytes 24584 | tf_op jit(solution)/shard_map/ppermute | solution.py:15
  103.8 49.1 %collective-permute-start.9 = (f32[18,1,128]{2,1,0:T(1,128)S(1)}, f32[18,1,128]{2,1,0:T(1,128)S(1)}, u32[]{:S(2)}, u32[]{:S(2)}) collective-permute-start(f32[18,1,128]{2,1,0:T(1,128)S(1)} %get-tuple-element.12), channel_id=1, source_target_pairs={{4,0},{5,1},{6,2},{7,3},{12,8},{13,9},{14,10},{15,11},{20,16},{21,... | collective-permute-start | bytes 27656 | tf_op jit(solution)/shard_map/ppermute | solution.py:18
  107.4 45.5 %collective-permute-start.8 = (f32[18,1,128]{2,1,0:T(1,128)S(1)}, f32[18,1,128]{2,1,0:T(1,128)S(1)}, u32[]{:S(2)}, u32[]{:S(2)}) collective-permute-start(f32[18,1,128]{2,1,0:T(1,128)S(1)} %get-tuple-element.11), channel_id=1, source_target_pairs={{0,4},{1,5},{2,6},{3,7},{8,12},{9,13},{10,14},{11,15},{16,20},{17,... | collective-permute-start | bytes 27656 | tf_op jit(solution)/shard_map/ppermute | solution.py:15
  152.8 9.7 %copy-start.11 = (f32[16]{0:T(128)S(1)}, f32[16]{0:T(128)}, u32[]{:S(2)}) copy-start(f32[16]{0:T(128)} %constant.160) | copy-start | bytes 196
  152.8 9.7 %copy-start.12 = (f32[16]{0:T(128)S(1)}, f32[16]{0:T(128)}, u32[]{:S(2)}) copy-start(f32[16]{0:T(128)} %constant.159) | copy-start | bytes 196
  153.0 5.4 %collective-permute-start.11 = (f32[18,18,1]{2,1,0:T(8,128)S(1)}, f32[18,18,1]{2,1,0:T(8,128)S(1)}, u32[]{:S(2)}, u32[]{:S(2)}) collective-permute-start(f32[18,18,1]{2,1,0:T(8,128)S(1)} %get-tuple-element.8), channel_id=1, source_target_pairs={{1,0},{2,1},{3,2},{5,4},{6,5},{7,6},{9,8},{10,9},{11,10},{13,12},{... | collective-permute-start | bytes 3896 | tf_op jit(solution)/shard_map/ppermute | solution.py:18
  155.0 7.3 %collective-permute-start.10 = (f32[18,18,1]{2,1,0:T(8,128)S(1)}, f32[18,18,1]{2,1,0:T(8,128)S(1)}, u32[]{:S(2)}, u32[]{:S(2)}) collective-permute-start(f32[18,18,1]{2,1,0:T(8,128)S(1)} %get-tuple-element.7), channel_id=1, source_target_pairs={{0,1},{1,2},{2,3},{4,5},{5,6},{6,7},{8,9},{9,10},{10,11},{12,13},{... | collective-permute-start | bytes 3896 | tf_op jit(solution)/shard_map/ppermute | solution.py:15
  162.6 0.7 copy-start.18
  (1 other events, 0.7 us)
where the time goes:
time: 165 us; the launch traced here: 164 us
  blocking collectives  85 us (52%)
  starting transfers between devices  27.8 us (17%)
  matrix products  14.7 us (9%)
  local copies, waits for them, and re-layouts  13.5 us (8%)
  waiting for transfers between devices  12.8 us (8%)
  other arithmetic  6.01 us (4%)
  between operations  4.12 us (2%)
    psum x1, blocking collectives, body(): curvature = lax.psum(jnp.sum(new_direction * image), ('gx', 'gy', 'gz'))  43.5 us
    psum x1, blocking collectives, body(): lax.psum((partial_inner, inner_local), ('gx', 'gy', 'gz'))  41.6 us
    ppermute x6, starting transfers between devices, padded_2(): lax.ppermute(lax.slice_in_dim(block, block.shape[dim] - width, None, axis...  15.4 us
    ppermute x6, starting transfers between devices, padded_2(): lax.ppermute(lax.slice_in_dim(block, 0, width, axis=dim), axis, backward)  12.4 us
    ppermute x6, waiting for transfers between devices, padded_2(): lax.ppermute(lax.slice_in_dim(block, block.shape[dim] - width, None, axis...  12.4 us
    gather x3, local copies, waits for them, and re-layouts, body(): jnp.take(extended_element, jnp.asarray(extended_index(elems_z)), axis=2)  3.9 us
  transfers between devices with their start and end apart: 12, of which 6 were waited for; matrix products, arithmetic and copies ran while one was open for 6% of the time, Pallas kernels for 0%

commit v1 on v0

v1 whole, which is shorter than its diff:
```python
import functools

import jax
import jax.numpy as jnp
import numpy as np
from jax import lax
from jax.experimental import pallas as pl
from jax.experimental.pallas import tpu as pltpu
from jax.sharding import PartitionSpec as P

MESH = pl.DeviceIdType.MESH
HIGHEST = lax.Precision.HIGHEST
F32 = jnp.float32
BF16 = jnp.bfloat16


def cheb_matrix():
    count = 8
    points = np.cos(np.pi * np.arange(count) / (count - 1))
    signs = np.array([2.0, 1, 1, 1, 1, 1, 1, 2.0]) * (-1.0) ** np.arange(count)
    differ = points[:, None] - points[None, :] + np.eye(count)
    matrix = np.outer(signs, 1.0 / signs) / differ
    matrix = matrix - np.eye(count) * np.sum(matrix, axis=1)[:, None]
    return (0.25 * matrix).astype(np.float32)


NN = (((1,), (0,)), ((), ()))
NT = (((1,), (1,)), ((), ()))
TN = (((0,), (0,)), ((), ()))


def split2(a):
    hi = a.astype(BF16)
    return hi, (a - hi.astype(F32)).astype(BF16)


def dot3(a, b, dims):
    ah, al = split2(a)
    bh, bl = b
    dot = lambda x, y: lax.dot_general(x, y, dims, preferred_element_type=F32)
    return dot(ah, bh) + (dot(ah, bl) + dot(al, bh))


def exact_dot(a, b, dims):
    return lax.dot_general(a, b, dims, precision=HIGHEST, preferred_element_type=F32)


def iota(shape, axis):
    return lax.broadcasted_iota(jnp.int32, shape, axis)


def group_stages(nx, ny, nz):
    if ny * nz <= 8:
        first = [(0, b, c) for b in range(ny) for c in range(nz) if (b, c) != (0, 0)]
        stages = [first]
    else:
        stages = [[(0, 0, c) for c in range(1, nz)], [(0, b, 0) for b in range(1, ny)]]
    return stages + [[(a, 0, 0) for a in range(1, nx)]]


def node_rows(elem, count, low, high):
    rows = [8 * elem - 2] + list(range(8 * elem, 8 * elem + 8)) + [8 * elem + 9]
    return [low if r < 0 else high if r >= 8 * count else r for r in rows]


def kernel(
    sizes,
    stages,
    res, sol, dirn, cond, mass, eb_s, eb, inv, idx, xv, xb, prior, dmat, dz,
    nsol, nres, ndir,
    zs, zr, q, ys, yr, ts, inv2, ws, lp, part, aslot, cin,
    zs2, zr2, g2, ys2, xr2, yr2, sc, bslot,
    hs, hr, as_, ar, bs_, br,
):
    nx, ny, nz = sizes
    ix, iy, iz = lax.axis_index("gx"), lax.axis_index("gy"), lax.axis_index("gz")
    D = cheb_matrix()
    have = {
        ("x", -1): ix > 0, ("x", 1): ix < nx - 1,
        ("y", -1): iy > 0, ("y", 1): iy < ny - 1,
        ("z", -1): iz > 0, ("z", 1): iz < nz - 1,
    }

    barrier = pltpu.get_barrier_semaphore()
    all_offsets = [o for stage in stages for o in stage]

    def partner(o):
        return (lax.rem(ix + o[0], nx), lax.rem(iy + o[1], ny), lax.rem(iz + o[2], nz))

    corners = {(a % nx, b % ny, 0) for a in (-1, 1) for b in (-1, 1)} - set(all_offsets) - {(0, 0, 0)}
    greeted = all_offsets + sorted(corners)
    for o in greeted:
        pl.semaphore_signal(barrier, inc=1, device_id=partner(o), device_id_type=MESH)

    def message(k, src, dst, dev):
        return pltpu.make_async_remote_copy(
            src_ref=src, dst_ref=dst, send_sem=hs.at[k], recv_sem=hr.at[k],
            device_id=dev, device_id_type=MESH,
        )

    def start(items):
        for send_if, recv_if, args in items:
            @pl.when(send_if)
            def _(args=args):
                message(*args).start()

    def wait_recv(items):
        for send_if, recv_if, args in items:
            @pl.when(recv_if)
            def _(args=args):
                message(*args).wait_recv()

    def wait_send(items):
        for send_if, recv_if, args in items:
            @pl.when(send_if)
            def _(args=args):
                message(*args).wait_send()

    def z_items(base, src, dst):
        return [
            (have["z", 1], have["z", -1], (base, src.at[1], dst.at[0], (ix, iy, iz + 1))),
            (have["z", -1], have["z", 1], (base + 1, src.at[0], dst.at[1], (ix, iy, iz - 1))),
        ]

    def face_items(base, x_src, x_dst, y_src, y_dst, lead):
        items = []
        for n, s in ((0, 1), (1, -1)):
            low = 0 if s == 1 else 1
            items.append((have["x", s], have["x", -s], (base + n, x_src[s], x_dst[-s], (ix + s, iy, iz))))
            near = (low,) + lead + (pl.ds(0, 16),)
            items.append((have["y", s], have["y", -s],
                          (base + 2 + n, y_src.at[(1 - low,)], y_dst.at[near], (ix, iy + s, iz))))
        k = base + 4
        for a in (1, -1):
            for b in (1, -1):
                rows = pl.ds(8, 8) if a == 1 else pl.ds(0, 8)
                drows = pl.ds(16, 8) if a == 1 else pl.ds(24, 8)
                side, dside = (1, 0) if b == 1 else (0, 1)
                items.append((have["x", a] & have["y", b], have["x", -a] & have["y", -b],
                              (k, y_src.at[(side,) + lead + (rows,)], y_dst.at[(dside,) + lead + (drows,)],
                               (ix + a, iy + b, iz))))
                k += 1
        return items

    full = (slice(None),)
    z1 = z_items(0, zs, zr)
    f1 = face_items(2, {1: q.at[14, pl.ds(0, 16)], -1: q.at[1, pl.ds(0, 16)]},
                    {-1: q.at[16, pl.ds(0, 16)], 1: q.at[17, pl.ds(0, 16)]}, ys, yr, ())
    z2 = z_items(10, zs2, zr2)
    f2 = face_items(12, {1: g2.at[:, 15], -1: g2.at[:, 0]}, {-1: xr2.at[0], 1: xr2.at[1]}, ys2, yr2, full)

    def ring(stage_no, src, slots, ss, rs):
        base = sum(len(s) for s in stages[:stage_no])
        return [
            pltpu.make_async_remote_copy(
                src_ref=src.at[stage_no], dst_ref=slots.at[base + n],
                send_sem=ss.at[base + n], recv_sem=rs.at[base + n],
                device_id=partner(o), device_id_type=MESH,
            )
            for n, o in enumerate(stages[stage_no])
        ]

    def ring_sum(stage_no, src, slots, copies):
        base = sum(len(s) for s in stages[:stage_no])
        total = src[stage_no]
        for n, c in enumerate(copies):
            c.wait_recv()
            total = total + slots[base + n]
        return total

    zero_z = jnp.zeros(zr.shape[1:], F32)
    zero_z2 = jnp.zeros(zr2.shape[1:], F32)
    for s, slot in ((-1, 0), (1, 1)):
        @pl.when(jnp.logical_not(have["z", s]))
        def _(slot=slot):
            zr[slot] = zero_z
            zr2[slot] = zero_z2

        @pl.when(jnp.logical_not(have["x", s]))
        def _(slot=slot):
            q[16 + slot, 0:16] = jnp.zeros((16, q.shape[2]), F32)
            xr2[slot] = jnp.zeros(xr2.shape[1:], F32)

        @pl.when(jnp.logical_not(have["y", s]))
        def _(slot=slot):
            yr[slot, 0:16] = jnp.zeros((16, yr.shape[2]), F32)
            yr2[slot, :, 0:16] = jnp.zeros((2, 16, yr2.shape[3]), F32)
    for a in (-1, 1):
        for b in (-1, 1):
            @pl.when(jnp.logical_not(have["x", a] & have["y", b]))
            def _(a=a, b=b):
                r = 16 if a == -1 else 24
                slot = 0 if b == -1 else 1
                yr[slot, r:r + 8] = jnp.zeros((8, yr.shape[2]), F32)
                yr2[slot, :, r:r + 8] = jnp.zeros((2, 8, yr2.shape[3]), F32)

    lanes = res.shape[2]
    wide = q.shape[2]
    r2d = res[...].reshape(256, lanes)
    rt = jnp.transpose(r2d)
    zs[0] = rt[0:8]
    zs[1] = rt[lanes - 8:lanes]

    elem_z = lanes // 8
    expand = (iota((elem_z, lanes), 1) // 8 == iota((elem_z, lanes), 0)).astype(BF16)
    coarse = xv.shape[1]
    masks = []
    acc = jnp.zeros((coarse, lanes), F32)
    for ex in range(2):
        for ey in range(2):
            ids = idx[ex, ey:ey + 1, :].astype(F32).astype(BF16)
            spread_ids = lax.dot_general(ids, expand, NN, preferred_element_type=F32)
            mask = spread_ids == iota((coarse, lanes), 0).astype(F32)
            masks.append(mask)
            block = res[8 * ex:8 * ex + 8, 8 * ey:8 * ey + 8, :]
            colsum = jnp.sum(jnp.sum(block, axis=0), axis=0, keepdims=True)
            acc = acc + jnp.where(mask, colsum, 0.0)
    coarse_res = jnp.sum(acc, axis=1, keepdims=True)
    nb = part.shape[1]
    partial = jnp.zeros((nb, xv.shape[2]), F32)
    rows_b = iota((nb, xv.shape[2]), 0)
    for k in range(xv.shape[0]):
        contrib = jnp.sum(xv[k] * coarse_res, axis=0, keepdims=True)
        partial = partial + jnp.where(rows_b == xb[k], contrib, 0.0)
    part[0] = partial

    pl.semaphore_wait(barrier, len(greeted))
    start(z1)
    a_copies = [ring(0, part, aslot, as_, ar)]
    for c in a_copies[0]:
        c.start()

    cols = iota((1, wide), 1)
    elem_of = sum((cols >= 10 * k).astype(jnp.int32) for k in range(1, elem_z))
    pick = (iota((10, wide), 0) == cols - 10 * elem_of).astype(F32)
    bwide = exact_dot(eb[...], pick, NN)
    dist = iota((lanes, wide), 0) - 8 * elem_of
    inner_part = jnp.zeros((lanes, wide), F32)
    for i in range(1, 9):
        inner_part = jnp.where(dist == i - 1, bwide[i:i + 1], inner_part)
    zfwd = jnp.where(dist == -2, bwide[0:1], jnp.where(dist == 9, bwide[9:10], inner_part))
    zfwd = split2(zfwd)
    zinv = split2(inner_part)
    rows16 = iota((16, wide), 0)
    zhalo = jnp.where((rows16 == 6) & (cols < 10), bwide[0:1], 0.0)
    zhalo = jnp.where((rows16 == 9) & (cols >= wide - 10), bwide[9:10], zhalo)
    zhalo = split2(zhalo)
    ebt = exact_dot((iota((16, 10), 0) == iota((16, 10), 1)).astype(F32), eb[...], NT)

    own = dot3(r2d, zfwd, NN)
    inv2[...] = jnp.zeros(inv2.shape, F32)
    for ey in range(2):
        inv2[:, ey, 0:10, :] = inv[:, 10 * ey:10 * ey + 10, :]

    wait_recv(z1)
    halo = jnp.concatenate([zr[0], zr[1]], axis=0)
    qv = (own + dot3(jnp.transpose(halo), zhalo, NN)).reshape(16, 16, wide)
    q[0:16, 0:16, :] = qv
    ys[0] = qv[:, 1, :]
    ys[1] = qv[:, 14, :]
    start(f1)

    dzs = split2(dz[...])

    def local_op(v):
        v4 = v.reshape(2, 8, 16, lanes)
        planes = [v4[:, j] for j in range(8)]
        cg = []
        for a in range(8):
            g = planes[0] * float(D[a, 0])
            for j in range(1, 8):
                g = g + planes[j] * float(D[a, j])
            cg.append(g * cond[0].reshape(2, 8, 16, lanes)[:, a])
        outs = []
        for i in range(8):
            o = cg[0] * float(D[0, i])
            for a in range(1, 8):
                o = o + cg[a] * float(D[a, i])
            outs.append(o)
        total = jnp.stack(outs, axis=1).reshape(16, 16, lanes) + mass[...] * v
        vy = v.reshape(16, 2, 8, lanes)
        g = vy[:, :, 0:1, :] * dmat[:, 0:1]
        for j in range(1, 8):
            g = g + vy[:, :, j:j + 1, :] * dmat[:, j:j + 1]
        g = g * cond[1].reshape(16, 2, 8, lanes)
        o = g[:, :, 0:1, :] * dmat[:, 8:9]
        for j in range(1, 8):
            o = o + g[:, :, j:j + 1, :] * dmat[:, 8 + j:9 + j]
        total = total + o.reshape(16, 16, lanes)
        gz = dot3(v.reshape(256, lanes), dzs, NT) * cond[2].reshape(256, lanes)
        return total + dot3(gz, dzs, NN).reshape(16, 16, lanes)

    dv = dirn[...]
    ld = local_op(dv)
    g2[1] = ld
    ldt = jnp.transpose(ld.reshape(256, lanes))
    zs2[0, 1] = ldt[0:8]
    zs2[1, 1] = ldt[lanes - 8:lanes]
    sc[0] = jnp.zeros((8, lanes), F32)
    sc[0, 2:3, :] = jnp.sum(jnp.sum(dv * ld, axis=0), axis=0, keepdims=True)

    for st in range(1, len(stages)):
        part[st] = ring_sum(st - 1, part, aslot, a_copies[st - 1])
        a_copies.append(ring(st, part, aslot, as_, ar))
        for c in a_copies[st]:
            c.start()

    wait_recv(f1)
    for s in range(2):
        q[0:16, 16 + s:17 + s, :] = yr[s, 0:16].reshape(16, 1, wide)
        q[16, 16 + s:17 + s, :] = yr[s, 22:23]
        q[17, 16 + s:17 + s, :] = yr[s, 25:26]
    for ey in range(2):
        t = None
        for j, row in enumerate(node_rows(ey, 2, 16, 17)):
            term = q[:, row:row + 1, :] * ebt[:, j:j + 1]
            t = term if t is None else t + term
        ts[:, ey] = t
    maps = [node_rows(ex, 2, 16, 17) for ex in range(2)]
    planes = [jnp.stack([ts[maps[0][i]], ts[maps[1][i]]]) for i in range(10)]
    inner_acc = None
    for a in range(10):
        u = planes[0] * eb_s[0, a]
        for i in range(1, 10):
            u = u + planes[i] * eb_s[i, a]
        w = u * jnp.stack([inv2[a], inv2[10 + a]])
        ws[a] = w
        term = u * w
        inner_acc = term if inner_acc is None else inner_acc + term
    inner_row = jnp.sum(jnp.sum(inner_acc, axis=(0, 1)), axis=0, keepdims=True)
    inner_local = jnp.sum(inner_row, axis=1, keepdims=True)
    sc[0, 3:4, :] = jnp.where(iota((1, lanes), 1) == 0, inner_local, 0.0)

    back = dot3(ws[...].reshape(640, wide), zinv, NT).reshape(10, 2, 2, 16, lanes)
    for m in range(8):
        o = back[0] * eb_s[m + 1, 0]
        for a in range(1, 10):
            o = o + back[a] * eb_s[m + 1, a]
        y = None
        for a in range(10):
            term = o[:, :, a:a + 1, :] * eb[1:9, a:a + 1]
            y = term if y is None else y + term
        lp[:, m] = y

    last = len(stages) - 1
    coarse_inner = ring_sum(last, part, aslot, a_copies[last])
    cin[...] = coarse_inner
    coarse_square = jnp.sum(jnp.sum(coarse_inner * coarse_inner, axis=0, keepdims=True), axis=1, keepdims=True)
    acc = None
    for k in range(xv.shape[0]):
        term = xv[k] * cin[pl.ds(xb[k], 1), :]
        acc = term if acc is None else acc + term
    coarse_sol = jnp.sum(acc, axis=1, keepdims=True)
    for ex in range(2):
        for ey in range(2):
            row = jnp.sum(jnp.where(masks[2 * ex + ey], coarse_sol, 0.0), axis=0, keepdims=True)
            lp[ex, :, ey] = lp[ex, :, ey] + row
    z = lp[...].reshape(16, 16, lanes)
    lz = local_op(z)
    lzt = jnp.transpose(lz.reshape(256, lanes))
    zs2[0, 0] = lzt[0:8]
    zs2[1, 0] = lzt[lanes - 8:lanes]
    start(z2)
    g2[0] = lz
    sc[0, 0:1, :] = jnp.sum(jnp.sum(z * lz, axis=0), axis=0, keepdims=True)
    sc[0, 1:2, :] = jnp.sum(jnp.sum(z * g2[1], axis=0), axis=0, keepdims=True)
    b_copies = [ring(0, sc, bslot, bs_, br)]
    for c in b_copies[0]:
        c.start()

    lane = iota((256, lanes), 1)
    up = (lane % 8 == 7) & (lane < lanes - 1)
    down = (lane % 8 == 0) & (lane > 0)
    r16 = iota((16, lanes), 0)
    l16 = iota((16, lanes), 1)
    put = (((r16 == 7) & (l16 == 0)) | ((r16 == 8) & (l16 == lanes - 1))).astype(F32)
    inside = []
    for n in range(2):
        v = g2[n].reshape(256, lanes)
        inside.append(v + jnp.where(up, pltpu.roll(v, lanes - 1, 1), 0.0) + jnp.where(down, pltpu.roll(v, 1, 1), 0.0))
    wait_recv(z2)
    for n in range(2):
        halo = jnp.concatenate([zr2[0, n], zr2[1, n]], axis=0)
        v = (inside[n] + exact_dot(jnp.transpose(halo), put, NN)).reshape(16, 16, lanes)
        g2[n] = v
        ys2[0, n] = v[:, 0, :]
        ys2[1, n] = v[:, 15, :]
    start(f2)
    for st in range(1, len(stages)):
        sc[st] = ring_sum(st - 1, sc, bslot, b_copies[st - 1])
        b_copies.append(ring(st, sc, bslot, bs_, br))
        for c in b_copies[st]:
            c.start()

    wait_recv(f2)
    sub = iota((16, lanes), 0)
    assembled = []
    for n in range(2):
        def along_y(v, low, high):
            return v + jnp.where(sub == 0, low, jnp.where(sub == 7, v[:, 8:9, :], jnp.where(
                sub == 8, v[:, 7:8, :], jnp.where(sub == 15, high, 0.0))))
        v = along_y(g2[n], yr2[0, n, 0:16].reshape(16, 1, lanes), yr2[1, n, 0:16].reshape(16, 1, lanes))
        xlo = along_y(xr2[0, n:n + 1], yr2[0, n, 23:24].reshape(1, 1, lanes), yr2[1, n, 23:24].reshape(1, 1, lanes))
        xhi = along_y(xr2[1, n:n + 1], yr2[0, n, 24:25].reshape(1, 1, lanes), yr2[1, n, 24:25].reshape(1, 1, lanes))
        assembled.append(jnp.concatenate([
            v[0:1] + xlo, v[1:7], v[7:8] + v[8:9], v[8:9] + v[7:8], v[9:15], v[15:16] + xhi], axis=0))

    total = ring_sum(last, sc, bslot, b_copies[last])
    sums = jnp.sum(total, axis=1, keepdims=True)
    inner = sums[3:4] + coarse_square
    ratio = inner / prior[0]
    curvature = sums[0:1] + 2.0 * ratio * sums[1:2] + ratio * ratio * sums[2:3]
    alpha = inner / curvature
    p = lp[...].reshape(16, 16, lanes) + ratio.reshape(1, 1, 1) * dirn[...]
    ndir[...] = p
    nsol[...] = sol[...] + alpha.reshape(1, 1, 1) * p
    nres[...] = res[...] - alpha.reshape(1, 1, 1) * (assembled[0] + ratio.reshape(1, 1, 1) * assembled[1])

    wait_send(z1 + f1 + z2 + f2)
    for copies in a_copies + b_copies:
        for c in copies:
            c.wait_send()


def body(sizes, residual, solution, direction, conductance, mass_term, eigen_basis, inverse_eigen_sums,
         element_coarse_index, xxt_values, xxt_blocks, prior_inner):
    stages = group_stages(*sizes)
    sends = sum(len(s) for s in stages)
    lanes = residual.shape[2]
    wide = inverse_eigen_sums.shape[2]
    coarse = xxt_values.shape[1]
    bs = xxt_values.shape[2]
    nb = coarse * sizes[0] * sizes[1] * sizes[2] // bs
    base = cheb_matrix()
    dmat = jnp.asarray(np.concatenate([base, base.T], axis=1))
    dz = jnp.asarray(np.kron(np.eye(lanes // 8, dtype=np.float32), base))
    vmem = pl.BlockSpec(memory_space=pltpu.VMEM)
    smem = pl.BlockSpec(memory_space=pltpu.SMEM)
    out = jax.ShapeDtypeStruct(residual.shape, F32)
    ns = len(stages)
    return pl.pallas_call(
        functools.partial(kernel, sizes, stages),
        out_shape=(out, out, out),
        in_specs=[vmem, vmem, vmem, vmem, vmem, smem, vmem, vmem, vmem, vmem, smem, smem, vmem, vmem],
        out_specs=(vmem, vmem, vmem),
        scratch_shapes=[
            pltpu.VMEM((2, 8, 256), F32),
            pltpu.VMEM((2, 8, 256), F32),
            pltpu.VMEM((18, 24, wide), F32),
            pltpu.VMEM((2, 16, wide), F32),
            pltpu.VMEM((2, 32, wide), F32),
            pltpu.VMEM((18, 2, 16, wide), F32),
            pltpu.VMEM((20, 2, 16, wide), F32),
            pltpu.VMEM((10, 2, 2, 16, wide), F32),
            pltpu.VMEM((2, 8, 2, 8, lanes), F32),
            pltpu.VMEM((ns, nb, bs), F32),
            pltpu.VMEM((sends, nb, bs), F32),
            pltpu.VMEM((nb, bs), F32),
            pltpu.VMEM((2, 2, 8, 256), F32),
            pltpu.VMEM((2, 2, 8, 256), F32),
            pltpu.VMEM((2, 16, 16, lanes), F32),
            pltpu.VMEM((2, 2, 16, lanes), F32),
            pltpu.VMEM((2, 2, 16, lanes), F32),
            pltpu.VMEM((2, 2, 32, lanes), F32),
            pltpu.VMEM((ns, 8, lanes), F32),
            pltpu.VMEM((sends, 8, lanes), F32),
            pltpu.SemaphoreType.DMA((20,)),
            pltpu.SemaphoreType.DMA((20,)),
            pltpu.SemaphoreType.DMA((sends,)),
            pltpu.SemaphoreType.DMA((sends,)),
            pltpu.SemaphoreType.DMA((sends,)),
            pltpu.SemaphoreType.DMA((sends,)),
        ],
        compiler_params=pltpu.CompilerParams(
            collective_id=0, has_side_effects=True, vmem_limit_bytes=48 * 1024 * 1024
        ),
    )(residual, solution, direction, conductance, mass_term, eigen_basis, eigen_basis, inverse_eigen_sums,
      element_coarse_index, xxt_values, xxt_blocks, prior_inner, dmat, dz)


def solution(mesh):
    grid = P("gx", "gy", "gz")
    in_specs = (
        grid, grid, grid, P(None, "gx", "gy", "gz"), grid, P(), grid, grid,
        P(("gx", "gy", "gz"), None, None), P(("gx", "gy", "gz")), P(),
    )
    sizes = (mesh.shape["gx"], mesh.shape["gy"], mesh.shape["gz"])
    return jax.shard_map(functools.partial(body, sizes), mesh=mesh, in_specs=in_specs,
                         out_specs=(grid, grid, grid), check_vma=False)
```

time: 165 us -> 35.5 us (0.22)
  the two profiles are of different devices: /device:TPU:6 before, /device:TPU:0 now
where the time goes in v1:
time: 35.5 us; the launch traced here: 35 us
  Pallas kernels  22.2 us (63%)
  local copies, waits for them, and re-layouts  11.5 us (32%)
  between operations  1.34 us (4%)
    pallas_call x1, Pallas kernels, body(): pl.pallas_call(functools.partial(kernel, sizes, stages), out_shape=(out,...  22.2 us
    unnamed x27, local copies, waits for them, and re-layouts  11.5 us

profile of v1, /device:TPU:0, one launch (start us, length us, event | category | flops | bytes accessed | tf_op | source)
XLA Modules:
  0.0 35.0 jit_solution(16149477462025575194)
XLA Ops:
  0.6 0.0 copy-start.11
  1.3 0.0 copy-done.11
  1.3 0.0 copy-start
  1.3 1.0 %copy-done = f32[20,20,160]{2,1,0:T(8,128)S(1)} copy-done((f32[20,20,160]{2,1,0:T(8,128)S(1)}, f32[20,20,160]{2,1,0:T(8,128)}, u32[]{:S(2)}) %copy-start) | copy-done | bytes 256024
  2.3 0.0 copy-start.1
  2.3 1.0 %copy-done.1 = f32[3,16,16,128]{3,2,1,0:T(8,128)S(1)} copy-done((f32[3,16,16,128]{3,2,1,0:T(8,128)S(1)}, f32[3,16,16,128]{3,2,1,0:T(8,128)}, u32[]{:S(2)}) %copy-start.1) | copy-done | bytes 393240
  3.3 0.0 copy-start.2
  3.3 0.9 %copy-done.2 = f32[8,64,128]{2,1,0:T(8,128)S(1)} copy-done((f32[8,64,128]{2,1,0:T(8,128)S(1)}, f32[8,64,128]{2,1,0:T(8,128)}, u32[]{:S(2)}) %copy-start.2) | copy-done | bytes 262168
  4.3 0.0 copy-start.3
  4.3 0.9 %copy-done.3 = f32[16,16,128]{2,1,0:T(8,128)S(1)} copy-done((f32[16,16,128]{2,1,0:T(8,128)S(1)}, f32[16,16,128]{2,1,0:T(8,128)}, u32[]{:S(2)}) %copy-start.3) | copy-done | bytes 131096
  5.2 0.0 copy-start.4
  5.2 0.9 %copy-done.4 = f32[16,16,128]{2,1,0:T(8,128)S(1)} copy-done((f32[16,16,128]{2,1,0:T(8,128)S(1)}, f32[16,16,128]{2,1,0:T(8,128)}, u32[]{:S(2)}) %copy-start.4) | copy-done | bytes 131096
  6.1 0.0 copy-start.5
  6.1 0.9 %copy-done.5 = f32[16,16,128]{2,1,0:T(8,128)S(1)} copy-done((f32[16,16,128]{2,1,0:T(8,128)S(1)}, f32[16,16,128]{2,1,0:T(8,128)}, u32[]{:S(2)}) %copy-start.5) | copy-done | bytes 131096
  7.0 0.0 copy-start.6
  7.0 0.9 %copy-done.6 = f32[16,16,128]{2,1,0:T(8,128)S(1)} copy-done((f32[16,16,128]{2,1,0:T(8,128)S(1)}, f32[16,16,128]{2,1,0:T(8,128)}, u32[]{:S(2)}) %copy-start.6) | copy-done | bytes 131096
  7.9 0.0 copy-start.7
  7.9 0.8 %copy-done.7 = f32[128,128]{1,0:T(8,128)S(1)} copy-done((f32[128,128]{1,0:T(8,128)S(1)}, f32[128,128]{1,0:T(8,128)}, u32[]{:S(2)}) %copy-start.7) | copy-done | bytes 65560
  8.8 0.0 copy-start.8
  8.8 0.7 %copy-done.8 = f32[10,10]{1,0:T(8,128)S(1)} copy-done((f32[10,10]{1,0:T(8,128)S(1)}, f32[10,10]{1,0:T(8,128)}, u32[]{:S(2)}) %copy-start.8) | copy-done | bytes 424
  9.4 0.0 copy-start.9
  9.4 0.7 %copy-done.9 = f32[8,16]{1,0:T(8,128)S(1)} copy-done((f32[8,16]{1,0:T(8,128)S(1)}, f32[8,16]{1,0:T(8,128)}, u32[]{:S(2)}) %copy-start.9) | copy-done | bytes 536
  10.1 0.0 copy-start.10
  10.1 0.7 %copy-done.10 = s32[2,2,16]{2,1,0:T(2,128)S(1)} copy-done((s32[2,2,16]{2,1,0:T(2,128)S(1)}, s32[2,2,16]{2,1,0:T(2,128)}, u32[]{:S(2)}) %copy-start.10) | copy-done | bytes 280
  10.8 22.2 %shard_map.148 = (f32[16,16,128]{2,1,0:T(8,128)S(1)}, f32[16,16,128]{2,1,0:T(8,128)S(1)}, f32[16,16,128]{2,1,0:T(8,128)S(1)}) custom-call(f32[16,16,128]{2,1,0:T(8,128)S(1)} %copy-done.3, f32[16,16,128]{2,1,0:T(8,128)S(1)} %copy-done.4, f32[16,16,128]{2,1,0:T(8,128)S(1)} %copy-done.5, f32[3,16,16,128]{3,2,1,0:T(8,128)S(1)} %copy-done.1, ...), custom_call_target="tpu_custom_call" | custom-call | tf_op jit(solution)/shard_map/pallas_call | solution.py:441
  33.1 0.7 %copy.20 = f32[16,16,128]{2,1,0:T(8,128)} copy(f32[16,16,128]{2,1,0:T(8,128)S(1)} %get-tuple-element.6) | data formatting | bytes 262144
  33.7 0.7 %copy.21 = f32[16,16,128]{2,1,0:T(8,128)} copy(f32[16,16,128]{2,1,0:T(8,128)S(1)} %get-tuple-element.7) | data formatting | bytes 262144
  34.4 0.7 %copy.22 = f32[16,16,128]{2,1,0:T(8,128)} copy(f32[16,16,128]{2,1,0:T(8,128)S(1)} %get-tuple-element.8) | data formatting | bytes 262144
Async XLA Ops:
  0.6 0.7 %copy-start.11 = (s32[8]{0:T(128)S(1)}, s32[8]{0:T(128)}, u32[]{:S(2)}) copy-start(s32[8]{0:T(128)} %xb.1) | copy-start | bytes 100
  1.3 1.0 %copy-start = (f32[20,20,160]{2,1,0:T(8,128)S(1)}, f32[20,20,160]{2,1,0:T(8,128)}, u32[]{:S(2)}) copy-start(f32[20,20,160]{2,1,0:T(8,128)} %inv.1) | copy-start | bytes 768004
  2.3 1.0 %copy-start.1 = (f32[3,16,16,128]{3,2,1,0:T(8,128)S(1)}, f32[3,16,16,128]{3,2,1,0:T(8,128)}, u32[]{:S(2)}) copy-start(f32[3,16,16,128]{3,2,1,0:T(8,128)} %cond.1) | copy-start | bytes 1179652
  3.3 0.9 %copy-start.2 = (f32[8,64,128]{2,1,0:T(8,128)S(1)}, f32[8,64,128]{2,1,0:T(8,128)}, u32[]{:S(2)}) copy-start(f32[8,64,128]{2,1,0:T(8,128)} %xv.1) | copy-start | bytes 786436
  4.3 0.9 %copy-start.3 = (f32[16,16,128]{2,1,0:T(8,128)S(1)}, f32[16,16,128]{2,1,0:T(8,128)}, u32[]{:S(2)}) copy-start(f32[16,16,128]{2,1,0:T(8,128)} %res.1) | copy-start | bytes 393220
  5.2 0.9 %copy-start.4 = (f32[16,16,128]{2,1,0:T(8,128)S(1)}, f32[16,16,128]{2,1,0:T(8,128)}, u32[]{:S(2)}) copy-start(f32[16,16,128]{2,1,0:T(8,128)} %sol.1) | copy-start | bytes 393220
  6.1 0.9 %copy-start.5 = (f32[16,16,128]{2,1,0:T(8,128)S(1)}, f32[16,16,128]{2,1,0:T(8,128)}, u32[]{:S(2)}) copy-start(f32[16,16,128]{2,1,0:T(8,128)} %dirn.1) | copy-start | bytes 393220
  7.0 0.9 %copy-start.6 = (f32[16,16,128]{2,1,0:T(8,128)S(1)}, f32[16,16,128]{2,1,0:T(8,128)}, u32[]{:S(2)}) copy-start(f32[16,16,128]{2,1,0:T(8,128)} %mass.1) | copy-start | bytes 393220
  7.9 0.8 %copy-start.7 = (f32[128,128]{1,0:T(8,128)S(1)}, f32[128,128]{1,0:T(8,128)}, u32[]{:S(2)}) copy-start(f32[128,128]{1,0:T(8,128)} %constant.5.clone.dz) | copy-start | bytes 196612
  8.8 0.7 %copy-start.8 = (f32[10,10]{1,0:T(8,128)S(1)}, f32[10,10]{1,0:T(8,128)}, u32[]{:S(2)}) copy-start(f32[10,10]{1,0:T(8,128)} %eb.1) | copy-start | bytes 1204
  9.4 0.7 %copy-start.9 = (f32[8,16]{1,0:T(8,128)S(1)}, f32[8,16]{1,0:T(8,128)}, u32[]{:S(2)}) copy-start(f32[8,16]{1,0:T(8,128)} %constant.4.clone.dmat) | copy-start | bytes 1540
  10.1 0.7 %copy-start.10 = (s32[2,2,16]{2,1,0:T(2,128)S(1)}, s32[2,2,16]{2,1,0:T(2,128)}, u32[]{:S(2)}) copy-start(s32[2,2,16]{2,1,0:T(2,128)} %idx.1) | copy-start | bytes 772

commit v2 on v1

--- a/solution.py
+++ b/solution.py
@@ -66,11 +66,12 @@
 def kernel(
     sizes,
     stages,
-    res, sol, dirn, cond, mass, eb_s, eb, inv, idx, xv, xb, prior, dmat, dz,
-    nsol, nres, ndir,
+    h_res, h_sol, h_dirn, h_cond, h_mass, h_eb, h_inv, h_idx, h_xv, h_xb, h_prior, h_dmat, h_dz,
+    o_sol, o_res, o_dir,
+    res, sol, dirn, cond, mass, eb, inv, idx, xv, xb, prior, dmat, dz, eb_s,
     zs, zr, q, ys, yr, ts, inv2, ws, lp, part, aslot, cin,
     zs2, zr2, g2, ys2, xr2, yr2, sc, bslot,
-    hs, hr, as_, ar, bs_, br,
+    nsol, nres, ndir, hs, hr, as_, ar, bs_, br, ls, os_,
 ):
     nx, ny, nz = sizes
     ix, iy, iz = lax.axis_index("gx"), lax.axis_index("gy"), lax.axis_index("gz")
@@ -81,6 +82,17 @@
         ("z", -1): iz > 0, ("z", 1): iz < nz - 1,
     }
 
+    pairs = dict(
+        res=(h_res, res), eb=(h_eb, eb), eb_s=(h_eb, eb_s), xv=(h_xv, xv), idx=(h_idx, idx), xb=(h_xb, xb),
+        dirn=(h_dirn, dirn), cond=(h_cond, cond), mass=(h_mass, mass), dmat=(h_dmat, dmat), dz=(h_dz, dz),
+        inv=(h_inv, inv), sol=(h_sol, sol), prior=(h_prior, prior),
+    )
+    loads = {name: pltpu.make_async_copy(src, dst, ls.at[n]) for n, (name, (src, dst)) in enumerate(pairs.items())}
+
+    def arrived(*names):
+        for name in names:
+            loads[name].wait()
+
     barrier = pltpu.get_barrier_semaphore()
     all_offsets = [o for stage in stages for o in stage]
 
@@ -91,6 +103,9 @@
     greeted = all_offsets + sorted(corners)
     for o in greeted:
         pl.semaphore_signal(barrier, inc=1, device_id=partner(o), device_id_type=MESH)
+
+    for copy in loads.values():
+        copy.start()
 
     def message(k, src, dst, dev):
         return pltpu.make_async_remote_copy(
@@ -196,12 +211,32 @@
 
     lanes = res.shape[2]
     wide = q.shape[2]
+    elem_z = lanes // 8
+    arrived("eb")
+    cols = iota((1, wide), 1)
+    elem_of = sum((cols >= 10 * k).astype(jnp.int32) for k in range(1, elem_z))
+    pick = (iota((10, wide), 0) == cols - 10 * elem_of).astype(F32)
+    bwide = exact_dot(eb[...], pick, NN)
+    dist = iota((lanes, wide), 0) - 8 * elem_of
+    inner_part = jnp.zeros((lanes, wide), F32)
+    for i in range(1, 9):
+        inner_part = jnp.where(dist == i - 1, bwide[i:i + 1], inner_part)
+    zfwd = jnp.where(dist == -2, bwide[0:1], jnp.where(dist == 9, bwide[9:10], inner_part))
+    zfwd = split2(zfwd)
+    zinv = split2(inner_part)
+    rows16 = iota((16, wide), 0)
+    zhalo = jnp.where((rows16 == 6) & (cols < 10), bwide[0:1], 0.0)
+    zhalo = jnp.where((rows16 == 9) & (cols >= wide - 10), bwide[9:10], zhalo)
+    zhalo = split2(zhalo)
+    ebt = exact_dot((iota((16, 10), 0) == iota((16, 10), 1)).astype(F32), eb[...], NT)
+
+    arrived("res")
     r2d = res[...].reshape(256, lanes)
     rt = jnp.transpose(r2d)
     zs[0] = rt[0:8]
     zs[1] = rt[lanes - 8:lanes]
 
-    elem_z = lanes // 8
+    arrived("idx", "xv", "xb")
     expand = (iota((elem_z, lanes), 1) // 8 == iota((elem_z, lanes), 0)).astype(BF16)
     coarse = xv.shape[1]
     masks = []
@@ -230,24 +265,8 @@
     for c in a_copies[0]:
         c.start()
 
-    cols = iota((1, wide), 1)
-    elem_of = sum((cols >= 10 * k).astype(jnp.int32) for k in range(1, elem_z))
-    pick = (iota((10, wide), 0) == cols - 10 * elem_of).astype(F32)
-    bwide = exact_dot(eb[...], pick, NN)
-    dist = iota((lanes, wide), 0) - 8 * elem_of
-    inner_part = jnp.zeros((lanes, wide), F32)
-    for i in range(1, 9):
-        inner_part = jnp.where(dist == i - 1, bwide[i:i + 1], inner_part)
-    zfwd = jnp.where(dist == -2, bwide[0:1], jnp.where(dist == 9, bwide[9:10], inner_part))
-    zfwd = split2(zfwd)
-    zinv = split2(inner_part)
-    rows16 = iota((16, wide), 0)
-    zhalo = jnp.where((rows16 == 6) & (cols < 10), bwide[0:1], 0.0)
-    zhalo = jnp.where((rows16 == 9) & (cols >= wide - 10), bwide[9:10], zhalo)
-    zhalo = split2(zhalo)
-    ebt = exact_dot((iota((16, 10), 0) == iota((16, 10), 1)).astype(F32), eb[...], NT)
-
     own = dot3(r2d, zfwd, NN)
+    arrived("inv")
     inv2[...] = jnp.zeros(inv2.shape, F32)
     for ey in range(2):
         inv2[:, ey, 0:10, :] = inv[:, 10 * ey:10 * ey + 10, :]
@@ -260,6 +279,7 @@
     ys[1] = qv[:, 14, :]
     start(f1)
 
+    arrived("dz", "dirn", "cond", "mass", "dmat")
     dzs = split2(dz[...])
 
     def local_op(v):
@@ -305,6 +325,7 @@
         for c in a_copies[st]:
             c.start()
 
+    arrived("eb_s", "sol", "prior")
     wait_recv(f1)
     for s in range(2):
         q[0:16, 16 + s:17 + s, :] = yr[s, 0:16].reshape(16, 1, wide)
@@ -413,13 +434,28 @@
     alpha = inner / curvature
     p = lp[...].reshape(16, 16, lanes) + ratio.reshape(1, 1, 1) * dirn[...]
     ndir[...] = p
+    saves = [pltpu.make_async_copy(src, dst, os_.at[n]) for n, (src, dst) in enumerate(
+        ((nsol, o_sol), (nres, o_res), (ndir, o_dir)))]
+    saves[2].start()
     nsol[...] = sol[...] + alpha.reshape(1, 1, 1) * p
+    saves[0].start()
     nres[...] = res[...] - alpha.reshape(1, 1, 1) * (assembled[0] + ratio.reshape(1, 1, 1) * assembled[1])
 
+    saves[1].start()
     wait_send(z1 + f1 + z2 + f2)
     for copies in a_copies + b_copies:
         for c in copies:
             c.wait_send()
+    for copy in saves:
+        copy.wait()
+
+
+def write_out(a, b, c, ao, bo, co, sems):
+    copies = [pltpu.make_async_copy(src, dst, sems.at[n]) for n, (src, dst) in enumerate(((a, ao), (b, bo), (c, co)))]
+    for copy in copies:
+        copy.start()
+    for copy in copies:
+        copy.wait()
 
 
 def body(sizes, residual, solution, direction, conductance, mass_term, eigen_basis, inverse_eigen_sums,
@@ -434,16 +470,20 @@
     base = cheb_matrix()
     dmat = jnp.asarray(np.concatenate([base, base.T], axis=1))
     dz = jnp.asarray(np.kron(np.eye(lanes // 8, dtype=np.float32), base))
-    vmem = pl.BlockSpec(memory_space=pltpu.VMEM)
-    smem = pl.BlockSpec(memory_space=pltpu.SMEM)
+    hbm = pl.BlockSpec(memory_space=pltpu.HBM)
     out = jax.ShapeDtypeStruct(residual.shape, F32)
     ns = len(stages)
-    return pl.pallas_call(
+    inputs = (residual, solution, direction, conductance, mass_term, eigen_basis, inverse_eigen_sums,
+              element_coarse_index, xxt_values, xxt_blocks, prior_inner, dmat, dz)
+    scalars = (9, 10)
+    held = [(pltpu.SMEM if n in scalars else pltpu.VMEM)(a.shape, a.dtype) for n, a in enumerate(inputs)]
+    results = pl.pallas_call(
         functools.partial(kernel, sizes, stages),
         out_shape=(out, out, out),
-        in_specs=[vmem, vmem, vmem, vmem, vmem, smem, vmem, vmem, vmem, vmem, smem, smem, vmem, vmem],
-        out_specs=(vmem, vmem, vmem),
-        scratch_shapes=[
+        in_specs=[hbm] * len(inputs),
+        out_specs=(hbm, hbm, hbm),
+        scratch_shapes=held + [
+            pltpu.SMEM(eigen_basis.shape, F32),
             pltpu.VMEM((2, 8, 256), F32),
             pltpu.VMEM((2, 8, 256), F32),
             pltpu.VMEM((18, 24, wide), F32),
@@ -464,18 +504,30 @@
             pltpu.VMEM((2, 2, 32, lanes), F32),
             pltpu.VMEM((ns, 8, lanes), F32),
             pltpu.VMEM((sends, 8, lanes), F32),
+            pltpu.VMEM(residual.shape, F32),
+            pltpu.VMEM(residual.shape, F32),
+            pltpu.VMEM(residual.shape, F32),
             pltpu.SemaphoreType.DMA((20,)),
             pltpu.SemaphoreType.DMA((20,)),
             pltpu.SemaphoreType.DMA((sends,)),
             pltpu.SemaphoreType.DMA((sends,)),
             pltpu.SemaphoreType.DMA((sends,)),
             pltpu.SemaphoreType.DMA((sends,)),
+            pltpu.SemaphoreType.DMA((len(inputs) + 1,)),
+            pltpu.SemaphoreType.DMA((3,)),
         ],
         compiler_params=pltpu.CompilerParams(
-            collective_id=0, has_side_effects=True, vmem_limit_bytes=48 * 1024 * 1024
+            collective_id=0, has_side_effects=True, vmem_limit_bytes=64 * 1024 * 1024
         ),
-    )(residual, solution, direction, conductance, mass_term, eigen_basis, eigen_basis, inverse_eigen_sums,
-      element_coarse_index, xxt_values, xxt_blocks, prior_inner, dmat, dz)
+    )(*inputs)
+    return pl.pallas_call(
+        write_out,
+        out_shape=(out, out, out),
+        in_specs=[hbm] * 3,
+        out_specs=(hbm, hbm, hbm),
+        scratch_shapes=[pltpu.SemaphoreType.DMA((3,))],
+        compiler_params=pltpu.CompilerParams(vmem_limit_bytes=64 * 1024 * 1024),
+    )(*results)
 
 
 def solution(mesh):

time: 35.5 us -> 36.9 us (1.039)
  Pallas kernels: 22.2 us -> 35.4 us
  local copies, waits for them, and re-layouts: 11.5 us -> 0 us
    pallas_call x0 -> x1, Pallas kernels: none -> 13 us  [body(): pl.pallas_call(write_out, out_shape=(out, out, out), in_specs=[hbm] * 3,...]
    unnamed x27 -> x0, local copies, waits for them, and re-layouts: 11.5 us -> none
where the time goes in v2:
time: 36.9 us; the launch traced here: 36.7 us
  Pallas kernels  35.4 us (96%)
  between operations  1.29 us (3%)
    pallas_call x1, Pallas kernels, body(): pl.pallas_call(functools.partial(kernel, sizes, stages), out_shape=(out,...  22.4 us
    pallas_call x1, Pallas kernels, body(): pl.pallas_call(write_out, out_shape=(out, out, out), in_specs=[hbm] * 3,...  13 us

profile of v2, /device:TPU:0, one launch (start us, length us, event | category | flops | bytes accessed | tf_op | source)
XLA Modules:
  0.0 36.7 jit_solution(5982934440960771604)
XLA Ops:
  1.3 22.4 %shard_map.148 = (f32[16,16,128]{2,1,0:T(8,128)}, f32[16,16,128]{2,1,0:T(8,128)}, f32[16,16,128]{2,1,0:T(8,128)}) custom-call(f32[16,16,128]{2,1,0:T(8,128)} %h_res.1, f32[16,16,128]{2,1,0:T(8,128)} %h_sol.1, f32[16,16,128]{2,1,0:T(8,128)} %h_dirn.1, f32[3,16,16,128]{3,2,1,0:T(8,128)} %h_cond.1, f32[16,16,128]{2,1,0:T(8,128)} %h_mass.1, f32[10,10]{1,0:T(8,128)} %h_eb.1, ...), custom_call_target="tpu_custom_call" | custom-call | tf_op jit(solution)/shard_map/pallas_call | solution.py:480
  23.7 13.0 %shard_map.149 = (f32[16,16,128]{2,1,0:T(8,128)}, f32[16,16,128]{2,1,0:T(8,128)}, f32[16,16,128]{2,1,0:T(8,128)}) custom-call(f32[16,16,128]{2,1,0:T(8,128)} %get-tuple-element.6.a, f32[16,16,128]{2,1,0:T(8,128)} %get-tuple-element.7.b, f32[16,16,128]{2,1,0:T(8,128)} %get-tuple-element.8.c), custom_call_target="tpu_custom_call" | custom-call | tf_op jit(solution)/shard_map/pallas_call | solution.py:523

commit v3 on v2

--- a/solution.py
+++ b/solution.py
@@ -113,49 +113,61 @@
             device_id=dev, device_id_type=MESH,
         )
 
-    def start(items):
-        for send_if, recv_if, args in items:
-            @pl.when(send_if)
-            def _(args=args):
-                message(*args).start()
-
-    def wait_recv(items):
-        for send_if, recv_if, args in items:
-            @pl.when(recv_if)
-            def _(args=args):
-                message(*args).wait_recv()
-
-    def wait_send(items):
-        for send_if, recv_if, args in items:
-            @pl.when(send_if)
-            def _(args=args):
-                message(*args).wait_send()
+    def each(items, act):
+        for args in items[None]:
+            act(message(*args))
+        if len(items) == 1:
+            return
+        for side in (-1, 1):
+            @pl.when(have["x", side])
+            def _(side=side):
+                for args in items[side]:
+                    act(message(*args))
+
+    def both(send, receive):
+        return {"send": send, "receive": receive}
+
+    def start(group):
+        each(group["send"], lambda m: m.start())
+
+    def wait_recv(group):
+        each(group["receive"], lambda m: m.wait_recv())
+
+    def wait_send(group):
+        each(group["send"], lambda m: m.wait_send())
+
+    up_y, down_y = lax.rem(iy + 1, ny), lax.rem(iy + ny - 1, ny)
+    up_z, down_z = lax.rem(iz + 1, nz), lax.rem(iz + nz - 1, nz)
 
     def z_items(base, src, dst):
-        return [
-            (have["z", 1], have["z", -1], (base, src.at[1], dst.at[0], (ix, iy, iz + 1))),
-            (have["z", -1], have["z", 1], (base + 1, src.at[0], dst.at[1], (ix, iy, iz - 1))),
-        ]
+        items = [(base, src.at[1], dst.at[0], (ix, iy, up_z)), (base + 1, src.at[0], dst.at[1], (ix, iy, down_z))]
+        return both({None: items}, {None: items})
 
     def face_items(base, x_src, x_dst, y_src, y_dst, lead):
-        items = []
-        for n, s in ((0, 1), (1, -1)):
-            low = 0 if s == 1 else 1
-            items.append((have["x", s], have["x", -s], (base + n, x_src[s], x_dst[-s], (ix + s, iy, iz))))
-            near = (low,) + lead + (pl.ds(0, 16),)
-            items.append((have["y", s], have["y", -s],
-                          (base + 2 + n, y_src.at[(1 - low,)], y_dst.at[near], (ix, iy + s, iz))))
-        k = base + 4
-        for a in (1, -1):
-            for b in (1, -1):
-                rows = pl.ds(8, 8) if a == 1 else pl.ds(0, 8)
-                drows = pl.ds(16, 8) if a == 1 else pl.ds(24, 8)
-                side, dside = (1, 0) if b == 1 else (0, 1)
-                items.append((have["x", a] & have["y", b], have["x", -a] & have["y", -b],
-                              (k, y_src.at[(side,) + lead + (rows,)], y_dst.at[(dside,) + lead + (drows,)],
-                               (ix + a, iy + b, iz))))
+        if ny == 2:
+            ways = [(1 - iy, iy, up_y)]
+        else:
+            ways = [(1, 0, up_y), (0, 1, down_y)]
+        send = {None: [], -1: [], 1: []}
+        receive = {None: [], -1: [], 1: []}
+        k = base
+        for side, slot, near in ways:
+            item = (k, y_src.at[side], y_dst.at[(slot,) + lead + (pl.ds(0, 16),)], (ix, near, iz))
+            send[None].append(item)
+            receive[None].append(item)
+            k += 1
+        for s in (1, -1):
+            item = (k, x_src[s], x_dst[-s], (ix + s, iy, iz))
+            send[s].append(item)
+            receive[-s].append(item)
+            k += 1
+            rows, drows = (pl.ds(8, 8), pl.ds(16, 8)) if s == 1 else (pl.ds(0, 8), pl.ds(24, 8))
+            for side, slot, near in ways:
+                item = (k, y_src.at[(side,) + lead + (rows,)], y_dst.at[(slot,) + lead + (drows,)], (ix + s, near, iz))
+                send[s].append(item)
+                receive[-s].append(item)
                 k += 1
-        return items
+        return both(send, receive)
 
     full = (slice(None),)
     z1 = z_items(0, zs, zr)
@@ -183,31 +195,8 @@
             total = total + slots[base + n]
         return total
 
-    zero_z = jnp.zeros(zr.shape[1:], F32)
-    zero_z2 = jnp.zeros(zr2.shape[1:], F32)
-    for s, slot in ((-1, 0), (1, 1)):
-        @pl.when(jnp.logical_not(have["z", s]))
-        def _(slot=slot):
-            zr[slot] = zero_z
-            zr2[slot] = zero_z2
-
-        @pl.when(jnp.logical_not(have["x", s]))
-        def _(slot=slot):
-            q[16 + slot, 0:16] = jnp.zeros((16, q.shape[2]), F32)
-            xr2[slot] = jnp.zeros(xr2.shape[1:], F32)
-
-        @pl.when(jnp.logical_not(have["y", s]))
-        def _(slot=slot):
-            yr[slot, 0:16] = jnp.zeros((16, yr.shape[2]), F32)
-            yr2[slot, :, 0:16] = jnp.zeros((2, 16, yr2.shape[3]), F32)
-    for a in (-1, 1):
-        for b in (-1, 1):
-            @pl.when(jnp.logical_not(have["x", a] & have["y", b]))
-            def _(a=a, b=b):
-                r = 16 if a == -1 else 24
-                slot = 0 if b == -1 else 1
-                yr[slot, r:r + 8] = jnp.zeros((8, yr.shape[2]), F32)
-                yr2[slot, :, r:r + 8] = jnp.zeros((2, 8, yr2.shape[3]), F32)
+    def or_zero(there, value):
+        return jnp.where(there, value, 0.0)
 
     lanes = res.shape[2]
     wide = q.shape[2]
@@ -272,7 +261,7 @@
         inv2[:, ey, 0:10, :] = inv[:, 10 * ey:10 * ey + 10, :]
 
     wait_recv(z1)
-    halo = jnp.concatenate([zr[0], zr[1]], axis=0)
+    halo = jnp.concatenate([or_zero(have["z", -1], zr[0]), or_zero(have["z", 1], zr[1])], axis=0)
     qv = (own + dot3(jnp.transpose(halo), zhalo, NN)).reshape(16, 16, wide)
     q[0:16, 0:16, :] = qv
     ys[0] = qv[:, 1, :]
@@ -327,10 +316,12 @@
 
     arrived("eb_s", "sol", "prior")
     wait_recv(f1)
-    for s in range(2):
-        q[0:16, 16 + s:17 + s, :] = yr[s, 0:16].reshape(16, 1, wide)
-        q[16, 16 + s:17 + s, :] = yr[s, 22:23]
-        q[17, 16 + s:17 + s, :] = yr[s, 25:26]
+    for n, s in enumerate((-1, 1)):
+        q[16 + n, 0:16] = or_zero(have["x", s], q[16 + n, 0:16])
+        there = have["y", s]
+        q[0:16, 16 + n:17 + n, :] = or_zero(there, yr[n, 0:16]).reshape(16, 1, wide)
+        q[16, 16 + n:17 + n, :] = or_zero(there & have["x", -1], yr[n, 22:23])
+        q[17, 16 + n:17 + n, :] = or_zero(there & have["x", 1], yr[n, 25:26])
     for ey in range(2):
         t = None
         for j, row in enumerate(node_rows(ey, 2, 16, 17)):
@@ -401,7 +392,7 @@
         inside.append(v + jnp.where(up, pltpu.roll(v, lanes - 1, 1), 0.0) + jnp.where(down, pltpu.roll(v, 1, 1), 0.0))
     wait_recv(z2)
     for n in range(2):
-        halo = jnp.concatenate([zr2[0, n], zr2[1, n]], axis=0)
+        halo = jnp.concatenate([or_zero(have["z", -1], zr2[0, n]), or_zero(have["z", 1], zr2[1, n])], axis=0)
         v = (inside[n] + exact_dot(jnp.transpose(halo), put, NN)).reshape(16, 16, lanes)
         g2[n] = v
         ys2[0, n] = v[:, 0, :]
@@ -420,9 +411,12 @@
         def along_y(v, low, high):
             return v + jnp.where(sub == 0, low, jnp.where(sub == 7, v[:, 8:9, :], jnp.where(
                 sub == 8, v[:, 7:8, :], jnp.where(sub == 15, high, 0.0))))
-        v = along_y(g2[n], yr2[0, n, 0:16].reshape(16, 1, lanes), yr2[1, n, 0:16].reshape(16, 1, lanes))
-        xlo = along_y(xr2[0, n:n + 1], yr2[0, n, 23:24].reshape(1, 1, lanes), yr2[1, n, 23:24].reshape(1, 1, lanes))
-        xhi = along_y(xr2[1, n:n + 1], yr2[0, n, 24:25].reshape(1, 1, lanes), yr2[1, n, 24:25].reshape(1, 1, lanes))
+        ends = [or_zero(have["y", s], yr2[m, n]) for m, s in enumerate((-1, 1))]
+        v = along_y(g2[n], ends[0][0:16].reshape(16, 1, lanes), ends[1][0:16].reshape(16, 1, lanes))
+        xlo = along_y(xr2[0, n:n + 1], ends[0][23:24].reshape(1, 1, lanes), ends[1][23:24].reshape(1, 1, lanes))
+        xhi = along_y(xr2[1, n:n + 1], ends[0][24:25].reshape(1, 1, lanes), ends[1][24:25].reshape(1, 1, lanes))
+        xlo = or_zero(have["x", -1], xlo)
+        xhi = or_zero(have["x", 1], xhi)
         assembled.append(jnp.concatenate([
             v[0:1] + xlo, v[1:7], v[7:8] + v[8:9], v[8:9] + v[7:8], v[9:15], v[15:16] + xhi], axis=0))
 
@@ -442,7 +436,8 @@
     nres[...] = res[...] - alpha.reshape(1, 1, 1) * (assembled[0] + ratio.reshape(1, 1, 1) * assembled[1])
 
     saves[1].start()
-    wait_send(z1 + f1 + z2 + f2)
+    for group in (z1, f1, z2, f2):
+        wait_send(group)
     for copies in a_copies + b_copies:
         for c in copies:
             c.wait_send()
@@ -450,11 +445,15 @@
         copy.wait()
 
 
-def write_out(a, b, c, ao, bo, co, sems):
-    copies = [pltpu.make_async_copy(src, dst, sems.at[n]) for n, (src, dst) in enumerate(((a, ao), (b, bo), (c, co)))]
-    for copy in copies:
+def write_out(a, b, c, ao, bo, co, held, load_sems, save_sems):
+    loads = [pltpu.make_async_copy(src, held.at[n], load_sems.at[n]) for n, src in enumerate((a, b, c))]
+    saves = [pltpu.make_async_copy(held.at[n], dst, save_sems.at[n]) for n, dst in enumerate((ao, bo, co))]
+    for copy in loads:
         copy.start()
-    for copy in copies:
+    for load, save in zip(loads, saves):
+        load.wait()
+        save.start()
+    for copy in saves:
         copy.wait()
 
 
@@ -525,7 +524,8 @@
         out_shape=(out, out, out),
         in_specs=[hbm] * 3,
         out_specs=(hbm, hbm, hbm),
-        scratch_shapes=[pltpu.SemaphoreType.DMA((3,))],
+        scratch_shapes=[pltpu.VMEM((3,) + residual.shape, F32), pltpu.SemaphoreType.DMA((3,)),
+                        pltpu.SemaphoreType.DMA((3,))],
         compiler_params=pltpu.CompilerParams(vmem_limit_bytes=64 * 1024 * 1024),
     )(*results)
 

time: 36.9 us -> 25.6 us (0.69)
  Pallas kernels: 35.4 us -> 24.1 us
    pallas_call x1, Pallas kernels: 13 us -> 1.74 us  [body(): pl.pallas_call(write_out, out_shape=(out, out, out), in_specs=[hbm] * 3,...]
where the time goes in v3:
time: 25.6 us; the launch traced here: 25.4 us
  Pallas kernels  24.1 us (94%)
  between operations  1.29 us (5%)
    pallas_call x1, Pallas kernels, body(): pl.pallas_call(functools.partial(kernel, sizes, stages), out_shape=(out,...  22.4 us
    pallas_call x1, Pallas kernels, body(): pl.pallas_call(write_out, out_shape=(out, out, out), in_specs=[hbm] * 3,...  1.74 us

profile of v3, /device:TPU:0, one launch (start us, length us, event | category | flops | bytes accessed | tf_op | source)
XLA Modules:
  0.0 25.4 jit_solution(6386608716814829748)
XLA Ops:
  1.3 22.4 %shard_map.148 = (f32[16,16,128]{2,1,0:T(8,128)}, f32[16,16,128]{2,1,0:T(8,128)}, f32[16,16,128]{2,1,0:T(8,128)}) custom-call(f32[16,16,128]{2,1,0:T(8,128)} %h_res.1, f32[16,16,128]{2,1,0:T(8,128)} %h_sol.1, f32[16,16,128]{2,1,0:T(8,128)} %h_dirn.1, f32[3,16,16,128]{3,2,1,0:T(8,128)} %h_cond.1, f32[16,16,128]{2,1,0:T(8,128)} %h_mass.1, f32[10,10]{1,0:T(8,128)} %h_eb.1, ...), custom_call_target="tpu_custom_call" | custom-call | tf_op jit(solution)/shard_map/pallas_call | solution.py:479
  23.7 1.7 %shard_map.149 = (f32[16,16,128]{2,1,0:T(8,128)}, f32[16,16,128]{2,1,0:T(8,128)}, f32[16,16,128]{2,1,0:T(8,128)}) custom-call(f32[16,16,128]{2,1,0:T(8,128)} %get-tuple-element.6.a, f32[16,16,128]{2,1,0:T(8,128)} %get-tuple-element.7.b, f32[16,16,128]{2,1,0:T(8,128)} %get-tuple-element.8.c), custom_call_target="tpu_custom_call" | custom-call | tf_op jit(solution)/shard_map/pallas_call | solution.py:522

commit v4 on v3

--- a/solution.py
+++ b/solution.py
@@ -314,6 +314,13 @@
         for c in a_copies[st]:
             c.start()
 
+    for ey in range(2):
+        t = None
+        for jj, row in enumerate(node_rows(ey, 2, 16, 17)):
+            if row < 16:
+                term = q[0:16, row:row + 1, :] * ebt[:, jj:jj + 1]
+                t = term if t is None else t + term
+        ts[0:16, ey] = t
     arrived("eb_s", "sol", "prior")
     wait_recv(f1)
     for n, s in enumerate((-1, 1)):
@@ -323,11 +330,15 @@
         q[16, 16 + n:17 + n, :] = or_zero(there & have["x", -1], yr[n, 22:23])
         q[17, 16 + n:17 + n, :] = or_zero(there & have["x", 1], yr[n, 25:26])
     for ey in range(2):
-        t = None
-        for j, row in enumerate(node_rows(ey, 2, 16, 17)):
-            term = q[:, row:row + 1, :] * ebt[:, j:j + 1]
-            t = term if t is None else t + term
-        ts[:, ey] = t
+        rows = node_rows(ey, 2, 16, 17)
+        ends = None
+        for jj, row in enumerate(rows):
+            col = ebt[:, jj:jj + 1]
+            if row >= 16:
+                ts[0:16, ey] = ts[0:16, ey] + q[0:16, row:row + 1, :] * col
+            term = q[16:18, row:row + 1, :] * col
+            ends = term if ends is None else ends + term
+        ts[16:18, ey] = ends
     maps = [node_rows(ex, 2, 16, 17) for ex in range(2)]
     planes = [jnp.stack([ts[maps[0][i]], ts[maps[1][i]]]) for i in range(10)]
     inner_acc = None
@@ -385,7 +396,7 @@
     down = (lane % 8 == 0) & (lane > 0)
     r16 = iota((16, lanes), 0)
     l16 = iota((16, lanes), 1)
-    put = (((r16 == 7) & (l16 == 0)) | ((r16 == 8) & (l16 == lanes - 1))).astype(F32)
+    put = (((r16 == 7) & (l16 == 0)) | ((r16 == 8) & (l16 == lanes - 1))).astype(BF16)
     inside = []
     for n in range(2):
         v = g2[n].reshape(256, lanes)
@@ -393,7 +404,10 @@
     wait_recv(z2)
     for n in range(2):
         halo = jnp.concatenate([or_zero(have["z", -1], zr2[0, n]), or_zero(have["z", 1], zr2[1, n])], axis=0)
-        v = (inside[n] + exact_dot(jnp.transpose(halo), put, NN)).reshape(16, 16, lanes)
+        hh, hl = split2(jnp.transpose(halo))
+        placed = lax.dot_general(hh, put, NN, preferred_element_type=F32) + lax.dot_general(
+            hl, put, NN, preferred_element_type=F32)
+        v = (inside[n] + placed).reshape(16, 16, lanes)
         g2[n] = v
         ys2[0, n] = v[:, 0, :]
         ys2[1, n] = v[:, 15, :]

time: 25.6 us -> 25.6 us (level)
  no operation moved by 1% of the time
where the time goes in v4:
time: 25.6 us; the launch traced here: 25.4 us
  Pallas kernels  24.1 us (94%)
  between operations  1.29 us (5%)
    pallas_call x1, Pallas kernels, body(): pl.pallas_call(functools.partial(kernel, sizes, stages), out_shape=(out,...  22.4 us
    pallas_call x1, Pallas kernels, body(): pl.pallas_call(write_out, out_shape=(out, out, out), in_specs=[hbm] * 3,...  1.74 us

profile of v4, /device:TPU:0, one launch (start us, length us, event | category | flops | bytes accessed | tf_op | source)
XLA Modules:
  0.0 25.4 jit_solution(7259191635560434356)
XLA Ops:
  1.3 22.4 %shard_map.148 = (f32[16,16,128]{2,1,0:T(8,128)}, f32[16,16,128]{2,1,0:T(8,128)}, f32[16,16,128]{2,1,0:T(8,128)}) custom-call(f32[16,16,128]{2,1,0:T(8,128)} %h_res.1, f32[16,16,128]{2,1,0:T(8,128)} %h_sol.1, f32[16,16,128]{2,1,0:T(8,128)} %h_dirn.1, f32[3,16,16,128]{3,2,1,0:T(8,128)} %h_cond.1, f32[16,16,128]{2,1,0:T(8,128)} %h_mass.1, f32[10,10]{1,0:T(8,128)} %h_eb.1, ...), custom_call_target="tpu_custom_call" | custom-call | tf_op jit(solution)/shard_map/pallas_call | solution.py:493
  23.7 1.7 %shard_map.149 = (f32[16,16,128]{2,1,0:T(8,128)}, f32[16,16,128]{2,1,0:T(8,128)}, f32[16,16,128]{2,1,0:T(8,128)}) custom-call(f32[16,16,128]{2,1,0:T(8,128)} %get-tuple-element.6.a, f32[16,16,128]{2,1,0:T(8,128)} %get-tuple-element.7.b, f32[16,16,128]{2,1,0:T(8,128)} %get-tuple-element.8.c), custom_call_target="tpu_custom_call" | custom-call | tf_op jit(solution)/shard_map/pallas_call | solution.py:536
